TPU v7x, 32 devices: a whole 2x2x4 slice. The times are simulated.
32 devices in a mesh: kv: 2 (over x), seq: 16 (over z, y, core).
Axes of the slice: x: 2, y: 2, z: 4, core: 2. Of those that a mesh axis runs over, the one named last changes fastest.
Arguments:
- queries: bfloat16 [512, 1024], P(('kv', 'seq')), may hold values from -6 to 6
- out_grad: bfloat16 [512, 1024], P(('kv', 'seq')), may hold values from -768 to 768
- saved_out: bfloat16 [512, 1024], P(('kv', 'seq')), may hold values from -1.5 to 1.5
- saved_lse: float32 [512, 8], P(('kv', 'seq')), as said below
- video_keys: bfloat16 [4096, 256], P('seq', 'kv'), may hold values from -6 to 6
- video_values: bfloat16 [4096, 256], P('seq', 'kv'), may hold values from -6 to 6
Outputs:
- grad_queries: bfloat16 [512, 1024], P(('kv', 'seq'))
- grad_keys: bfloat16 [4096, 256], P('seq', 'kv')
- grad_values: bfloat16 [4096, 256], P('seq', 'kv')
Inputs may be any that keep to these rules, and one draw needn't show every extreme that they name: saved_lse lies between log(4096) and log(4096) + 1.5.
All inputs are finite; a program needn't handle non-finite values.
Results may differ from a plain program's by a relative error of at most 0.0057.
Values may be sent and summed in bfloat16 or wider, within the bound.
No kernel may reach another device: no remote copies, remote signals or barrier semaphores. Data moves between devices by JAX's collectives and lax.ppermute only.
A program may use at most 64 MiB of HBM per device.

v0:
```python
import functools
import math

import jax
import jax.numpy as jnp
from jax import lax
from jax.experimental import pallas as pl
from jax.experimental.pallas import tpu as pltpu
from jax.sharding import PartitionSpec as P

LANES = 128
PIECES = 3
VMEM_BYTES = 32 * 1024 * 1024


def vmem(count):
    return [pl.BlockSpec(memory_space=pltpu.VMEM)] * count


def bf16(value):
    return value.astype(jnp.bfloat16)


def f32(value):
    return value.astype(jnp.float32)


def pack_kernel(
    heads, groups, score_scale,
    queries, out_grad, saved_out, saved_lse, keys, values,
    rows_out, pairs_out, saved_block, lse_block, done,
):
    own_rows, width = queries.shape
    group_width = width // groups
    group_heads = heads // groups
    head_width = width // heads
    group = lax.axis_index("kv")
    moves = [(saved_lse, lse_block)]
    for step in range(groups):
        source = lax.rem(group + step, groups)
        columns = pl.ds(pl.multiple_of(source * group_width, group_width), group_width)
        target = step * group_width
        moves.append((out_grad.at[:, columns], rows_out.at[:, pl.ds(width + target, group_width)]))
        moves.append((saved_out.at[:, columns], saved_block.at[:, pl.ds(target, group_width)]))
    needed = len(moves)
    for step in range(groups):
        source = lax.rem(group + step, groups)
        columns = pl.ds(pl.multiple_of(source * group_width, group_width), group_width)
        moves.append((queries.at[:, columns], rows_out.at[:, pl.ds(step * group_width, group_width)]))
    moves.append((keys, pairs_out.at[:, pl.ds(0, head_width)]))
    moves.append((values, pairs_out.at[:, pl.ds(head_width, head_width)]))
    copies = [
        pltpu.make_async_copy(source, target, done.at[index])
        for index, (source, target) in enumerate(moves)
    ]
    for copy in copies:
        copy.start()
    lane = lax.broadcasted_iota(jnp.int32, (own_rows, LANES), 1)
    piece = lax.rem(lane, PIECES)
    stats = jnp.zeros((own_rows, LANES), jnp.float32)
    for copy in copies[:needed]:
        copy.wait()
    shifts = jnp.concatenate(
        [lse_block[...], jnp.zeros((heads, LANES - own_rows), jnp.float32)], axis=1
    ).T[:own_rows] * (1.0 / score_scale)
    for head in range(heads):
        columns = slice(head * head_width, (head + 1) * head_width)
        grad_columns = slice(width + head * head_width, width + (head + 1) * head_width)
        products = f32(rows_out[:, grad_columns]) * f32(saved_block[:, columns])
        delta = jnp.sum(products, axis=1, keepdims=True)
        place = (heads + head) * PIECES
        stats = jnp.where((lane >= place) & (lane < place + PIECES), delta, stats)
        place = lax.rem(head - group * group_heads + heads, heads) * PIECES
        stats = jnp.where((lane >= place) & (lane < place + PIECES), shifts[:, head : head + 1], stats)
    first = f32(bf16(stats))
    second = f32(bf16(stats - first))
    third = stats - first - second
    rows_out[:, 2 * width :] = bf16(jnp.where(piece == 0, first, jnp.where(piece == 1, second, third)))
    for copy in copies[needed:]:
        copy.wait()


def pack(queries, out_grad, saved_out, saved_lse, keys, values, groups, score_scale):
    own_rows, width = queries.shape
    heads = saved_lse.shape[0]
    return pl.pallas_call(
        functools.partial(pack_kernel, heads, groups, score_scale),
        out_shape=(
            jax.ShapeDtypeStruct((own_rows, 2 * width + LANES), jnp.bfloat16),
            jax.ShapeDtypeStruct((keys.shape[0], 2 * keys.shape[1]), jnp.bfloat16),
        ),
        in_specs=[pl.BlockSpec(memory_space=pltpu.HBM)] * 6,
        out_specs=tuple(vmem(2)),
        scratch_shapes=[
            pltpu.VMEM((own_rows, width), jnp.bfloat16),
            pltpu.VMEM(saved_lse.shape, jnp.float32),
            pltpu.SemaphoreType.DMA((3 * groups + 3,)),
        ],
        compiler_params=pltpu.CompilerParams(vmem_limit_bytes=VMEM_BYTES),
    )(*[
        pltpu.with_memory_space_constraint(array, pltpu.HBM)
        for array in (queries, out_grad, saved_out, saved_lse, keys, values)
    ])


def dot(left, right, left_dim, right_dim):
    return lax.dot_general(
        left, right, (((left_dim,), (right_dim,)), ((), ())), preferred_element_type=jnp.float32
    )


def attend_kernel(heads, groups, score_scale, arrays, order, pair_count, carried, *refs):
    refs = list(refs)
    held = [refs.pop(0) for _ in range(arrays)]
    pairs = [refs.pop(0) for _ in range(pair_count)]
    before = [refs.pop(0) for _ in range(pair_count)] if carried else None
    dq_own, dq_other, *dpairs = refs
    block_rows = held[0].shape[0]
    width = (held[0].shape[1] - LANES) // 2
    head_width = width // heads
    group_heads = heads // groups
    all_rows = len(order) * block_rows
    half = all_rows // 2
    rows = [held[array].at[pl.ds(place * block_rows, block_rows)] for array, place in order]
    key_rows = pairs[0].shape[0]
    per_group = pair_count // groups
    exponent = score_scale * math.log2(math.e)
    lane = lax.broadcasted_iota(jnp.int32, (all_rows, LANES), 1)
    stats = jnp.concatenate([block[:, 2 * width :] for block in rows], axis=0)
    none = jnp.zeros_like(stats)

    def stacked(start):
        return jnp.concatenate(
            [
                block[:, start + member * head_width : start + (member + 1) * head_width]
                for member in range(group_heads)
                for block in rows
            ],
            axis=0,
        )

    def picked(first):
        firsts = [first + member * PIECES for member in range(group_heads)]
        return jnp.concatenate(
            [jnp.where((lane >= place) & (lane < place + PIECES), stats, none) for place in firsts], axis=0
        )

    for group in range(groups):
        head = group * group_heads
        query = stacked(head * head_width)
        grad = stacked(width + head * head_width)
        query_wide = jnp.concatenate([query, picked(head * PIECES)], axis=1)
        grad_wide = jnp.concatenate([grad, picked((heads + head) * PIECES)], axis=1)
        members = range(group * per_group, (group + 1) * per_group)
        keys = jnp.concatenate([pairs[index][:, :head_width] for index in members], axis=0)
        values = jnp.concatenate([pairs[index][:, head_width:] for index in members], axis=0)
        minus = jnp.full(keys.shape, -1.0, jnp.bfloat16)
        scores = dot(jnp.concatenate([keys, minus], axis=1), query_wide, 1, 1)
        probs = jnp.exp2(scores * exponent)
        dprobs = dot(jnp.concatenate([values, minus], axis=1), grad_wide, 1, 1)
        dscores = bf16(probs * dprobs)
        dvalues = dot(bf16(probs), grad, 1, 0)
        dkeys = dot(dscores, query, 1, 0) * score_scale
        for place, index in enumerate(members):
            out = dpairs[index]
            taken = slice(place * key_rows, (place + 1) * key_rows)
            dkey, dvalue = dkeys[taken], dvalues[taken]
            if carried:
                dkey = dkey + before[index][:, :head_width]
                dvalue = dvalue + before[index][:, head_width:]
            out[:, :head_width] = dkey.astype(out.dtype)
            out[:, head_width:] = dvalue.astype(out.dtype)
        dquery = dot(keys, dscores, 0, 0).T * score_scale
        for member in range(group_heads):
            part = dquery[member * all_rows : (member + 1) * all_rows]
            columns = slice((head + member) * head_width, (head + member + 1) * head_width)
            dq_own[:, columns] = part[:half]
            dq_other[:, columns] = bf16(part[half:])


def attend(rows, order, pairs, before, kinds, heads, groups, score_scale):
    block_rows, packed = rows[0].shape
    width = (packed - LANES) // 2
    half = len(order) // 2 * block_rows
    key_rows, head_width = pairs[0].shape[0], pairs[0].shape[1] // 2
    outs = [
        jax.ShapeDtypeStruct((half, width), jnp.float32),
        jax.ShapeDtypeStruct((half, width), jnp.bfloat16),
    ] + [jax.ShapeDtypeStruct(pairs[0].shape, kind) for kind in kinds]
    operands = list(rows) + list(pairs) + list(before)
    products = len(pairs) * key_rows * (heads // groups) * 2 * half
    return pl.pallas_call(
        functools.partial(
            attend_kernel, heads, groups, score_scale, len(rows), order, len(pairs), bool(before)
        ),
        out_shape=tuple(outs),
        in_specs=vmem(len(operands)),
        out_specs=tuple(vmem(len(outs))),
        compiler_params=pltpu.CompilerParams(vmem_limit_bytes=VMEM_BYTES),
        cost_estimate=pl.CostEstimate(
            flops=10 * products * head_width, bytes_accessed=0, transcendentals=products
        ),
    )(*operands)


def finish_kernel(groups, terms, *refs):
    query_terms, pair_terms = refs[:terms], refs[terms : 2 * terms]
    grad_queries, grad_keys, grad_values, queries_block, keys_block, values_block, done = refs[2 * terms :]
    group = lax.axis_index("kv")
    group_width = queries_block.shape[1] // groups
    head_width = keys_block.shape[1]

    def total(parts, columns):
        return functools.reduce(lambda left, right: left + right, [f32(part[:, columns]) for part in parts])

    copies = []
    for block, target, columns in (
        (keys_block, grad_keys, slice(0, head_width)),
        (values_block, grad_values, slice(head_width, 2 * head_width)),
    ):
        block[...] = bf16(total(pair_terms, columns))
        copies.append(pltpu.make_async_copy(block, target, done.at[len(copies)]))
        copies[-1].start()
    for step in range(groups):
        columns = slice(step * group_width, (step + 1) * group_width)
        queries_block[:, columns] = bf16(total(query_terms, columns))
        target = lax.rem(group + step, groups) * group_width
        target = grad_queries.at[:, pl.ds(pl.multiple_of(target, group_width), group_width)]
        source = queries_block.at[:, pl.ds(step * group_width, group_width)]
        copies.append(pltpu.make_async_copy(source, target, done.at[len(copies)]))
        copies[-1].start()
    for copy in copies:
        copy.wait()


def finish(query_terms, pair_terms, groups):
    own_rows, width = query_terms[0].shape
    key_rows, head_width = pair_terms[0].shape[0], pair_terms[0].shape[1] // 2
    shapes = ((own_rows, width), (key_rows, head_width), (key_rows, head_width))
    operands = list(query_terms) + list(pair_terms)
    return pl.pallas_call(
        functools.partial(finish_kernel, groups, len(query_terms)),
        out_shape=tuple(pltpu.HBM(shape, jnp.bfloat16) for shape in shapes),
        in_specs=vmem(len(operands)),
        out_specs=tuple([pl.BlockSpec(memory_space=pltpu.HBM)] * 3),
        scratch_shapes=[pltpu.VMEM(shape, jnp.bfloat16) for shape in shapes]
        + [pltpu.SemaphoreType.DMA((groups + 2,))],
        compiler_params=pltpu.CompilerParams(vmem_limit_bytes=VMEM_BYTES),
    )(*operands)


def turn_seq(array, seq_count, target):
    return lax.ppermute(array, "seq", [(place, target(place)) for place in range(seq_count)])


def planes(queries, out_grad, saved_out, saved_lse, video_keys, video_values):
    groups = lax.axis_size("kv")
    seq_count = lax.axis_size("seq")
    own_rows, width = queries.shape
    heads = saved_lse.shape[1]
    head_width = video_keys.shape[1]
    score_scale = 1.0 / math.sqrt(head_width)

    def steps(array, even, odd):
        return turn_seq(array, seq_count, lambda place: place ^ (4 * (odd if place % 2 else even)))

    def other_core(array):
        return turn_seq(array, seq_count, lambda place: place ^ 1)

    def middle(array):
        return turn_seq(array, seq_count, lambda place: place ^ 2)

    def across(array):
        return lax.ppermute(array, "kv", [(0, 1), (1, 0)])

    def diagonal(array):
        steps = [
            (kv * seq_count + place, (1 - kv) * seq_count + (place ^ 2))
            for kv in range(2)
            for place in range(seq_count)
        ]
        return lax.ppermute(array, ("kv", "seq"), steps)

    packed, pair = pack(
        queries, out_grad, saved_out, saved_lse.T, video_keys, video_values, groups, score_scale
    )
    pair_across, pair_middle = across(pair), middle(pair)
    keys_far = middle(pair_across[:, :head_width])
    values_far = across(pair_middle[:, head_width:])
    pairs = [pair, pair_middle, pair_across, jnp.concatenate([keys_far, values_far], axis=1)]
    beside = other_core(packed)
    from_far = steps(packed, 3, 3)
    from_near = steps(jnp.concatenate([packed, beside], axis=0), 1, 2)
    rows = [packed, beside, from_near, other_core(from_near), from_far, other_core(from_far)]
    order = ((0, 0), (2, 0), (3, 1), (4, 0), (1, 0), (3, 0), (2, 1), (5, 0))
    kinds = [jnp.float32] + [jnp.bfloat16] * 3
    dq_own, dq_other, *dpairs = attend(rows, order, pairs, [], kinds, heads, groups, score_scale)
    parts = dpairs[1:]
    pair_terms = [dpairs[0]] + [send(parts[place]) for send, place in ((middle, 0), (across, 1), (diagonal, 2))]
    dq = (dq_own + f32(other_core(dq_other))).reshape(-1, own_rows, width)
    query_terms = [dq[0]] + [
        steps(bf16(dq[place]), even, odd) for place, even, odd in ((1, 1, 2), (2, 2, 1), (3, 3, 3))
    ]
    return finish(query_terms, pair_terms, groups)


def head_columns(block, first, width):
    return lax.dynamic_slice_in_dim(block, first, width, 1)


def seq_major(block, kv_count, seq_count):
    total_rows = block.shape[0]
    width = block.shape[1]
    shaped = block.reshape(kv_count, seq_count, total_rows // (kv_count * seq_count), width)
    return shaped.transpose(1, 0, 2, 3).reshape(total_rows, width)


def make_accumulate(
    lse_group,
    delta_group,
    group_index,
    group_width,
    group_heads,
    head_width,
    score_scale,
    video_keys,
    video_values,
):

    def accumulate(totals, pieces, offset):
        key_total, value_total, query_rows = totals
        query_block, grad_block = pieces
        query_block = head_columns(query_block, group_index * group_width, group_width)
        grad_block = head_columns(grad_block, group_index * group_width, group_width)
        columns = []
        for member in range(group_heads):
            query_head = query_block[:, member * head_width : (member + 1) * head_width]
            grad_head = grad_block[:, member * head_width : (member + 1) * head_width]
            scores = (
                jnp.einsum("nd,kd->nk", query_head, video_keys, preferred_element_type=jnp.float32)
                * score_scale
            )
            probs = jnp.exp(scores - lse_group[:, member : member + 1])
            probs_half = probs.astype(jnp.bfloat16)
            value_total = value_total + jnp.einsum(
                "nk,nd->kd", probs_half, grad_head, preferred_element_type=jnp.float32
            )
            dprobs = jnp.einsum(
                "nd,kd->nk", grad_head, video_values, preferred_element_type=jnp.float32
            )
            dscores = (probs * (dprobs - delta_group[:, member : member + 1])).astype(jnp.bfloat16)
            key_total = key_total + jnp.einsum(
                "nk,nd->kd", dscores, query_head, preferred_element_type=jnp.float32
            )
            columns.append(
                jnp.einsum("nk,kd->nd", dscores, video_keys, preferred_element_type=jnp.float32)
            )
        query_rows = jnp.concatenate(columns, axis=1)
        return (key_total, value_total, query_rows)

    return accumulate


def shards(queries, out_grad, saved_out, saved_lse, video_keys, video_values):
    kv_count = lax.axis_size("kv")
    seq_count = lax.axis_size("seq")
    group_index = lax.axis_index("kv")
    head_width = video_keys.shape[1]
    group_heads = saved_lse.shape[1] // kv_count
    group_width = group_heads * head_width
    own_rows = queries.shape[0]
    total_rows = own_rows * kv_count * seq_count
    score_scale = 1.0 / math.sqrt(head_width)
    products = out_grad.astype(jnp.float32) * saved_out.astype(jnp.float32)
    own_delta = products.reshape(own_rows, -1, head_width).sum(axis=2)
    lse_all, delta_all = (
        lax.all_gather(saved_lse, ("kv", "seq"), axis=0, tiled=True),
        lax.all_gather(own_delta, ("kv", "seq"), axis=0, tiled=True),
    )
    lse_wide = head_columns(lse_all, group_index * group_heads, group_heads)
    delta_wide = head_columns(delta_all, group_index * group_heads, group_heads)
    key_rows = video_keys.shape[0]
    initial = (
        jnp.zeros((key_rows, head_width), jnp.float32),
        jnp.zeros((key_rows, head_width), jnp.float32),
        jnp.zeros((total_rows, group_width), jnp.float32),
    )
    wide_step = make_accumulate(
        lse_wide,
        delta_wide,
        group_index,
        group_width,
        group_heads,
        head_width,
        score_scale,
        video_keys,
        video_values,
    )
    gathered = (
        lax.all_gather(queries, ("kv", "seq"), axis=0, tiled=True),
        lax.all_gather(out_grad, ("kv", "seq"), axis=0, tiled=True),
    )
    key_total, value_total, query_rows = wide_step(initial, gathered, 0)
    query_rows = seq_major(query_rows, kv_count, seq_count)
    summed = lax.psum_scatter(
        query_rows.reshape(seq_count, total_rows // seq_count, group_width),
        "seq",
        scatter_dimension=0,
        tiled=True,
    )
    rounded = (summed * score_scale).astype(jnp.bfloat16).reshape(kv_count, own_rows, group_width)
    returned = lax.all_to_all(rounded, "kv", split_axis=0, concat_axis=2, tiled=True)
    grad_queries = returned.reshape(own_rows, kv_count * group_width)
    return (
        grad_queries,
        (key_total * score_scale).astype(jnp.bfloat16),
        value_total.astype(jnp.bfloat16),
    )


def fits_planes(kv_count, seq_count, args):
    queries, _, _, saved_lse, video_keys, _ = args
    return (
        kv_count == 2
        and seq_count == 16
        and queries.shape[0] % 16 == 0
        and video_keys.shape[0] % 16 == 0
        and video_keys.shape[1] == LANES
        and 2 * PIECES * saved_lse.shape[1] <= LANES
    )


def program(*args):
    if fits_planes(lax.axis_size("kv"), lax.axis_size("seq"), args):
        return planes(*args)
    return shards(*args)


def solution(mesh):
    return jax.shard_map(
        program,
        mesh=mesh,
        in_specs=(
            P(("kv", "seq"), None),
            P(("kv", "seq"), None),
            P(("kv", "seq"), None),
            P(("kv", "seq"), None),
            P("seq", "kv"),
            P("seq", "kv"),
        ),
        out_specs=(P(("kv", "seq"), None), P("seq", "kv"), P("seq", "kv")),
        check_vma=False,
    )
```

profile of v0, /device:TPU:0, one launch (start us, length us, event | category | flops | bytes accessed | tf_op | source)
XLA Modules:
  0.0 30.7 jit_solution(11011272240897244044)
XLA Ops:
  0.6 1.2 %shard_map.85 = (bf16[16,2176]{1,0:T(8,128)(2,1)S(1)}, bf16[256,256]{1,0:T(8,128)(2,1)S(1)}) custom-call(bf16[16,1024]{1,0:T(8,128)(2,1)} %queries.1, bf16[16,1024]{1,0:T(8,128)(2,1)} %out_grad.1, bf16[16,1024]{1,0:T(8,128)(2,1)} %saved_out.1, f32[8,16]{1,0:T(8,128)} %bitcast.1, bf16[256,128]{1,0:T(8,128)(2,1)} %keys.1, bf16[256,128]{1,0:T(8,128)(2,1)} %values.1), custom_call_target="tpu_custom_call" | custom-call | tf_op jit(solution)/shard_map/pallas_call | solution.py:86
  1.8 0.5 %collective-permute-start = (bf16[16,2176]{1,0:T(8,128)(2,1)S(1)}, bf16[16,2176]{1,0:T(8,128)(2,1)S(1)}, u32[]{:S(2)}, u32[]{:S(2)}) collective-permute-start(bf16[16,2176]{1,0:T(8,128)(2,1)S(1)} %get-tuple-element.11.refs_0_), channel_id=1, source_target_pairs={{0,1},{1,0},{2,3},{3,2},{4,5},{5,4},{6,7},{7,6},{8,9},{9,8},{10,11... | collective-permute-start | bytes 208904 | tf_op jit(solution)/shard_map/ppermute | solution.py:253
  2.4 2.6 %collective-permute-start.6 = (bf16[256,256]{1,0:T(8,128)(2,1)S(1)}, bf16[256,256]{1,0:T(8,128)(2,1)S(1)}, u32[]{:S(2)}, u32[]{:S(2)}) collective-permute-start(bf16[256,256]{1,0:T(8,128)(2,1)S(1)} %get-tuple-element.12.refs_6_), channel_id=1, source_target_pairs={{0,16},{16,0},{1,17},{17,1},{2,18},{18,2},{3,19},{19,3},{4,20},{20... | collective-permute-start | bytes 393224 | tf_op jit(solution)/shard_map/ppermute | solution.py:274
  4.9 1.5 %collective-permute-start.5 = (bf16[256,256]{1,0:T(8,128)(2,1)S(1)}, bf16[256,256]{1,0:T(8,128)(2,1)S(1)}, u32[]{:S(2)}, u32[]{:S(2)}) collective-permute-start(bf16[256,256]{1,0:T(8,128)(2,1)S(1)} %get-tuple-element.12.refs_6_), channel_id=1, source_target_pairs={{0,2},{1,3},{2,0},{3,1},{4,6},{5,7},{6,4},{7,5},{8,10},{9,11},{10,... | collective-permute-start | bytes 393224 | tf_op jit(solution)/shard_map/ppermute | solution.py:253
  6.4 0.0 collective-permute-done.refs_1_
  6.5 1.6 %collective-permute-start.1 = (bf16[32,2176]{1,0:T(8,128)(2,1)S(1)}, bf16[32,2176]{1,0:T(8,128)(2,1)S(1)}, u32[]{:S(2)}, u32[]{:S(2)}) collective-permute-start(bf16[32,2176]{1,0:T(8,128)(2,1)S(1)} %pad_maximum_fusion), channel_id=1, source_target_pairs={{0,4},{1,9},{2,6},{3,11},{4,0},{5,13},{6,2},{7,15},{8,12},{9,1},{1... | collective-permute-start | bytes 417800 | tf_op jit(solution)/shard_map/ppermute | solution.py:253
  8.1 2.5 %collective-permute-start.3 = (bf16[16,2176]{1,0:T(8,128)(2,1)S(1)}, bf16[16,2176]{1,0:T(8,128)(2,1)S(1)}, u32[]{:S(2)}, u32[]{:S(2)}) collective-permute-start(bf16[16,2176]{1,0:T(8,128)(2,1)S(1)} %get-tuple-element.11.refs_0_), channel_id=1, source_target_pairs={{0,12},{1,13},{2,14},{3,15},{4,8},{5,9},{6,10},{7,11},{8,4},{9,5},... | collective-permute-start | bytes 208904 | tf_op jit(solution)/shard_map/ppermute | solution.py:253
  10.6 0.0 collective-permute-done.6.refs_8_
  10.6 0.6 %collective-permute-start.7 = (bf16[256,128]{1,0:T(8,128)(2,1)S(1)}, bf16[256,128]{1,0:T(8,128)(2,1)S(1)}, u32[]{:S(2)}, u32[]{:S(2)}) collective-permute-start(bf16[256,128]{1,0:T(8,128)(2,1)S(1)} %slice.31), channel_id=1, source_target_pairs={{0,2},{1,3},{2,0},{3,1},{4,6},{5,7},{6,4},{7,5},{8,10},{9,11},{10,... | collective-permute-start | bytes 196616 | tf_op jit(solution)/shard_map/ppermute | solution.py:253
  11.2 0.0 collective-permute-done.5.refs_7_
  11.2 1.2 %collective-permute-start.8 = (bf16[256,128]{1,0:T(8,128)(2,1)S(1)}, bf16[256,128]{1,0:T(8,128)(2,1)S(1)}, u32[]{:S(2)}, u32[]{:S(2)}) collective-permute-start(bf16[256,128]{1,0:T(8,128)(2,1)S(1)} %slice.32), channel_id=1, source_target_pairs={{0,16},{16,0},{1,17},{17,1},{2,18},{18,2},{3,19},{19,3},{4,20},{20... | collective-permute-start | bytes 196616 | tf_op jit(solution)/shard_map/ppermute | solution.py:274
  12.4 0.3 collective-permute-done.1.refs_2_
  12.6 0.5 %collective-permute-start.2 = (bf16[32,2176]{1,0:T(8,128)(2,1)S(1)}, bf16[32,2176]{1,0:T(8,128)(2,1)S(1)}, u32[]{:S(2)}, u32[]{:S(2)}) collective-permute-start(bf16[32,2176]{1,0:T(8,128)(2,1)S(1)} %collective-permute-done.1.refs_2_), channel_id=1, source_target_pairs={{0,1},{1,0},{2,3},{3,2},{4,5},{5,4},{6,7},{7,6},{8,9},{9,8},{10,11... | collective-permute-start | bytes 417800 | tf_op jit(solution)/shard_map/ppermute | solution.py:253
  13.1 2.4 %collective-permute-done.3.refs_4_ = bf16[16,2176]{1,0:T(8,128)(2,1)S(1)} collective-permute-done((bf16[16,2176]{1,0:T(8,128)(2,1)S(1)}, bf16[16,2176]{1,0:T(8,128)(2,1)S(1)}, u32[]{:S(2)}, u32[]{:S(2)}) %collective-permute-start.3) | collective-permute-done | bytes 69664 | tf_op jit(solution)/shard_map/ppermute | solution.py:253
  15.5 0.0 collective-permute-start.4
  15.5 0.0 collective-permute-done.7
  15.5 0.0 collective-permute-done.8
  15.5 1.2 %collective-permute-done.4.refs_5_ = bf16[16,2176]{1,0:T(8,128)(2,1)S(1)} collective-permute-done((bf16[16,2176]{1,0:T(8,128)(2,1)S(1)}, bf16[16,2176]{1,0:T(8,128)(2,1)S(1)}, u32[]{:S(2)}, u32[]{:S(2)}) %collective-permute-start.4) | collective-permute-done | bytes 69664 | tf_op jit(solution)/shard_map/ppermute | solution.py:253
  16.7 0.0 collective-permute-done.2.refs_3_
  16.8 1.6 %shard_map.86 = (f32[64,1024]{1,0:T(8,128)S(1)}, bf16[64,1024]{1,0:T(8,128)(2,1)S(1)}, f32[256,256]{1,0:T(8,128)S(1)}, bf16[256,256]{1,0:T(8,128)(2,1)S(1)}, bf1...) custom-call(bf16[16,2176]{1,0:T(8,128)(2,1)S(1)} %get-tuple-element.11.refs_0_, ...), custom_call_target="tpu_custom_call" | custom-call | flops 671088640 | tf_op jit(solution)/shard_map/pallas_call | solution.py:192
  18.4 0.2 collective-permute-start.9
  18.6 0.5 %collective-permute-start.13 = (bf16[256,256]{1,0:T(8,128)(2,1)S(1)}, bf16[256,256]{1,0:T(8,128)(2,1)S(1)}, u32[]{:S(2)}, u32[]{:S(2)}) collective-permute-start(bf16[256,256]{1,0:T(8,128)(2,1)S(1)} %get-tuple-element.16), channel_id=1, source_target_pairs={{0,2},{1,3},{2,0},{3,1},{4,6},{5,7},{6,4},{7,5},{8,10},{9,11},{10,... | collective-permute-start | bytes 393224 | tf_op jit(solution)/shard_map/ppermute | solution.py:253
  19.1 0.9 %collective-permute-start.14 = (bf16[256,256]{1,0:T(8,128)(2,1)S(1)}, bf16[256,256]{1,0:T(8,128)(2,1)S(1)}, u32[]{:S(2)}, u32[]{:S(2)}) collective-permute-start(bf16[256,256]{1,0:T(8,128)(2,1)S(1)} %get-tuple-element.17), channel_id=1, source_target_pairs={{0,16},{16,0},{1,17},{17,1},{2,18},{18,2},{3,19},{19,3},{4,20},{20... | collective-permute-start | bytes 393224 | tf_op jit(solution)/shard_map/ppermute | solution.py:274
  20.0 2.1 %collective-permute-start.15 = (bf16[256,256]{1,0:T(8,128)(2,1)S(1)}, bf16[256,256]{1,0:T(8,128)(2,1)S(1)}, u32[]{:S(2)}, u32[]{:S(2)}) collective-permute-start(bf16[256,256]{1,0:T(8,128)(2,1)S(1)} %get-tuple-element.18), channel_id=1, source_target_pairs={{0,18},{1,19},{2,16},{3,17},{4,22},{5,23},{6,20},{7,21},{8,26},{9,... | collective-permute-start | bytes 393224 | tf_op jit(solution)/shard_map/ppermute | solution.py:282
  22.1 0.0 collective-permute-done.9
  22.1 2.9 %collective-permute-start.12 = (bf16[16,1024]{1,0:T(8,128)(2,1)S(1)}, bf16[16,1024]{1,0:T(8,128)(2,1)S(1)}, u32[]{:S(2)}, u32[]{:S(2)}) collective-permute-start(bf16[16,1024]{1,0:T(8,128)(2,1)S(1)} %get-tuple-element.21), channel_id=1, source_target_pairs={{0,12},{1,13},{2,14},{3,15},{4,8},{5,9},{6,10},{7,11},{8,4},{9,5},... | collective-permute-start | bytes 98312 | tf_op jit(solution)/shard_map/ppermute | solution.py:253
  25.0 0.0 collective-permute-start.11
  25.0 0.0 collective-permute-done.13.refs_5_
  25.0 1.5 %collective-permute-start.10 = (bf16[16,1024]{1,0:T(8,128)(2,1)S(1)}, bf16[16,1024]{1,0:T(8,128)(2,1)S(1)}, u32[]{:S(2)}, u32[]{:S(2)}) collective-permute-start(bf16[16,1024]{1,0:T(8,128)(2,1)S(1)} %get-tuple-element.23), channel_id=1, source_target_pairs={{0,4},{1,9},{2,6},{3,11},{4,0},{5,13},{6,2},{7,15},{8,12},{9,1},{1... | collective-permute-start | bytes 98312 | tf_op jit(solution)/shard_map/ppermute | solution.py:253
  26.6 0.0 collective-permute-done.14.refs_6_
  26.6 1.7 %collective-permute-done.15.refs_7_ = bf16[256,256]{1,0:T(8,128)(2,1)S(1)} collective-permute-done((bf16[256,256]{1,0:T(8,128)(2,1)S(1)}, bf16[256,256]{1,0:T(8,128)(2,1)S(1)}, u32[]{:S(2)}, u32[]{:S(2)}) %collective-permute-start.15) | collective-permute-done | bytes 131104 | tf_op jit(solution)/shard_map/ppermute | solution.py:282
  28.3 0.0 collective-permute-done.12.refs_3_
  28.3 1.7 %collective-permute-done.11.refs_2_ = bf16[16,1024]{1,0:T(8,128)(2,1)S(1)} collective-permute-done((bf16[16,1024]{1,0:T(8,128)(2,1)S(1)}, bf16[16,1024]{1,0:T(8,128)(2,1)S(1)}, u32[]{:S(2)}, u32[]{:S(2)}) %collective-permute-start.11) | collective-permute-done | bytes 32800 | tf_op jit(solution)/shard_map/ppermute | solution.py:253
  30.0 0.0 collective-permute-done.10.refs_1_
  30.0 0.7 %shard_map.87 = (bf16[16,1024]{1,0:T(8,128)(2,1)}, bf16[256,128]{1,0:T(8,128)(2,1)}, bf16[256,128]{1,0:T(8,128)(2,1)}) custom-call(f32[16,1024]{1,0:T(8,128)S(1)} %slice.33.refs_0_, bf16[16,1024]{1,0:T(8,128)(2,1)S(1)} %collective-permute-done.10.refs_1_, bf16[16,1024]{1,0:T(8,128)(2,1)S(1)} %collective-permute-done.11.refs_2_, ...), custom_call_target="tpu_custom_call" | custom-call | tf_op jit(solution)/shard_map/pallas_call | solution.py:241
  (7 shorter events, 0.1 us)
Async XLA Ops:
  1.8 4.6 %collective-permute-start = (bf16[16,2176]{1,0:T(8,128)(2,1)S(1)}, bf16[16,2176]{1,0:T(8,128)(2,1)S(1)}, u32[]{:S(2)}, u32[]{:S(2)}) collective-permute-start(bf16[16,2176]{1,0:T(8,128)(2,1)S(1)} %get-tuple-element.11.refs_0_), channel_id=1, source_target_pairs={{0,1},{1,0},{2,3},{3,2},{4,5},{5,4},{6,7},{7,6},{8,9},{9,8},{10,11... | collective-permute-start | bytes 208904 | tf_op jit(solution)/shard_map/ppermute | solution.py:253
  2.4 8.2 %collective-permute-start.6 = (bf16[256,256]{1,0:T(8,128)(2,1)S(1)}, bf16[256,256]{1,0:T(8,128)(2,1)S(1)}, u32[]{:S(2)}, u32[]{:S(2)}) collective-permute-start(bf16[256,256]{1,0:T(8,128)(2,1)S(1)} %get-tuple-element.12.refs_6_), channel_id=1, source_target_pairs={{0,16},{16,0},{1,17},{17,1},{2,18},{18,2},{3,19},{19,3},{4,20},{20... | collective-permute-start | bytes 393224 | tf_op jit(solution)/shard_map/ppermute | solution.py:274
  4.9 6.2 %collective-permute-start.5 = (bf16[256,256]{1,0:T(8,128)(2,1)S(1)}, bf16[256,256]{1,0:T(8,128)(2,1)S(1)}, u32[]{:S(2)}, u32[]{:S(2)}) collective-permute-start(bf16[256,256]{1,0:T(8,128)(2,1)S(1)} %get-tuple-element.12.refs_6_), channel_id=1, source_target_pairs={{0,2},{1,3},{2,0},{3,1},{4,6},{5,7},{6,4},{7,5},{8,10},{9,11},{10,... | collective-permute-start | bytes 393224 | tf_op jit(solution)/shard_map/ppermute | solution.py:253
  6.5 6.2 %collective-permute-start.1 = (bf16[32,2176]{1,0:T(8,128)(2,1)S(1)}, bf16[32,2176]{1,0:T(8,128)(2,1)S(1)}, u32[]{:S(2)}, u32[]{:S(2)}) collective-permute-start(bf16[32,2176]{1,0:T(8,128)(2,1)S(1)} %pad_maximum_fusion), channel_id=1, source_target_pairs={{0,4},{1,9},{2,6},{3,11},{4,0},{5,13},{6,2},{7,15},{8,12},{9,1},{1... | collective-permute-start | bytes 417800 | tf_op jit(solution)/shard_map/ppermute | solution.py:253
  8.1 7.4 %collective-permute-start.3 = (bf16[16,2176]{1,0:T(8,128)(2,1)S(1)}, bf16[16,2176]{1,0:T(8,128)(2,1)S(1)}, u32[]{:S(2)}, u32[]{:S(2)}) collective-permute-start(bf16[16,2176]{1,0:T(8,128)(2,1)S(1)} %get-tuple-element.11.refs_0_), channel_id=1, source_target_pairs={{0,12},{1,13},{2,14},{3,15},{4,8},{5,9},{6,10},{7,11},{8,4},{9,5},... | collective-permute-start | bytes 208904 | tf_op jit(solution)/shard_map/ppermute | solution.py:253
  10.6 4.9 %collective-permute-start.7 = (bf16[256,128]{1,0:T(8,128)(2,1)S(1)}, bf16[256,128]{1,0:T(8,128)(2,1)S(1)}, u32[]{:S(2)}, u32[]{:S(2)}) collective-permute-start(bf16[256,128]{1,0:T(8,128)(2,1)S(1)} %slice.31), channel_id=1, source_target_pairs={{0,2},{1,3},{2,0},{3,1},{4,6},{5,7},{6,4},{7,5},{8,10},{9,11},{10,... | collective-permute-start | bytes 196616 | tf_op jit(solution)/shard_map/ppermute | solution.py:253
  11.2 4.3 %collective-permute-start.8 = (bf16[256,128]{1,0:T(8,128)(2,1)S(1)}, bf16[256,128]{1,0:T(8,128)(2,1)S(1)}, u32[]{:S(2)}, u32[]{:S(2)}) collective-permute-start(bf16[256,128]{1,0:T(8,128)(2,1)S(1)} %slice.32), channel_id=1, source_target_pairs={{0,16},{16,0},{1,17},{17,1},{2,18},{18,2},{3,19},{19,3},{4,20},{20... | collective-permute-start | bytes 196616 | tf_op jit(solution)/shard_map/ppermute | solution.py:274
  12.6 4.1 %collective-permute-start.2 = (bf16[32,2176]{1,0:T(8,128)(2,1)S(1)}, bf16[32,2176]{1,0:T(8,128)(2,1)S(1)}, u32[]{:S(2)}, u32[]{:S(2)}) collective-permute-start(bf16[32,2176]{1,0:T(8,128)(2,1)S(1)} %collective-permute-done.1.refs_2_), channel_id=1, source_target_pairs={{0,1},{1,0},{2,3},{3,2},{4,5},{5,4},{6,7},{7,6},{8,9},{9,8},{10,11... | collective-permute-start | bytes 417800 | tf_op jit(solution)/shard_map/ppermute | solution.py:253
  15.5 1.3 %collective-permute-start.4 = (bf16[16,2176]{1,0:T(8,128)(2,1)S(1)}, bf16[16,2176]{1,0:T(8,128)(2,1)S(1)}, u32[]{:S(2)}, u32[]{:S(2)}) collective-permute-start(bf16[16,2176]{1,0:T(8,128)(2,1)S(1)} %collective-permute-done.3.refs_4_), channel_id=1, source_target_pairs={{0,1},{1,0},{2,3},{3,2},{4,5},{5,4},{6,7},{7,6},{8,9},{9,8},{10,11... | collective-permute-start | bytes 208904 | tf_op jit(solution)/shard_map/ppermute | solution.py:253
  18.4 3.7 %collective-permute-start.9 = (bf16[64,1024]{1,0:T(8,128)(2,1)S(1)}, bf16[64,1024]{1,0:T(8,128)(2,1)S(1)}, u32[]{:S(2)}, u32[]{:S(2)}) collective-permute-start(bf16[64,1024]{1,0:T(8,128)(2,1)S(1)} %get-tuple-element.14), channel_id=1, source_target_pairs={{0,1},{1,0},{2,3},{3,2},{4,5},{5,4},{6,7},{7,6},{8,9},{9,8},{10,11... | collective-permute-start | bytes 393224 | tf_op jit(solution)/shard_map/ppermute | solution.py:253
  18.6 6.5 %collective-permute-start.13 = (bf16[256,256]{1,0:T(8,128)(2,1)S(1)}, bf16[256,256]{1,0:T(8,128)(2,1)S(1)}, u32[]{:S(2)}, u32[]{:S(2)}) collective-permute-start(bf16[256,256]{1,0:T(8,128)(2,1)S(1)} %get-tuple-element.16), channel_id=1, source_target_pairs={{0,2},{1,3},{2,0},{3,1},{4,6},{5,7},{6,4},{7,5},{8,10},{9,11},{10,... | collective-permute-start | bytes 393224 | tf_op jit(solution)/shard_map/ppermute | solution.py:253
  19.1 7.5 %collective-permute-start.14 = (bf16[256,256]{1,0:T(8,128)(2,1)S(1)}, bf16[256,256]{1,0:T(8,128)(2,1)S(1)}, u32[]{:S(2)}, u32[]{:S(2)}) collective-permute-start(bf16[256,256]{1,0:T(8,128)(2,1)S(1)} %get-tuple-element.17), channel_id=1, source_target_pairs={{0,16},{16,0},{1,17},{17,1},{2,18},{18,2},{3,19},{19,3},{4,20},{20... | collective-permute-start | bytes 393224 | tf_op jit(solution)/shard_map/ppermute | solution.py:274
  20.0 8.3 %collective-permute-start.15 = (bf16[256,256]{1,0:T(8,128)(2,1)S(1)}, bf16[256,256]{1,0:T(8,128)(2,1)S(1)}, u32[]{:S(2)}, u32[]{:S(2)}) collective-permute-start(bf16[256,256]{1,0:T(8,128)(2,1)S(1)} %get-tuple-element.18), channel_id=1, source_target_pairs={{0,18},{1,19},{2,16},{3,17},{4,22},{5,23},{6,20},{7,21},{8,26},{9,... | collective-permute-start | bytes 393224 | tf_op jit(solution)/shard_map/ppermute | solution.py:282
  22.1 6.2 %collective-permute-start.12 = (bf16[16,1024]{1,0:T(8,128)(2,1)S(1)}, bf16[16,1024]{1,0:T(8,128)(2,1)S(1)}, u32[]{:S(2)}, u32[]{:S(2)}) collective-permute-start(bf16[16,1024]{1,0:T(8,128)(2,1)S(1)} %get-tuple-element.21), channel_id=1, source_target_pairs={{0,12},{1,13},{2,14},{3,15},{4,8},{5,9},{6,10},{7,11},{8,4},{9,5},... | collective-permute-start | bytes 98312 | tf_op jit(solution)/shard_map/ppermute | solution.py:253
  25.0 5.0 %collective-permute-start.11 = (bf16[16,1024]{1,0:T(8,128)(2,1)S(1)}, bf16[16,1024]{1,0:T(8,128)(2,1)S(1)}, u32[]{:S(2)}, u32[]{:S(2)}) collective-permute-start(bf16[16,1024]{1,0:T(8,128)(2,1)S(1)} %get-tuple-element.22), channel_id=1, source_target_pairs={{0,8},{1,5},{2,10},{3,7},{4,12},{5,1},{6,14},{7,3},{8,0},{9,13},{1... | collective-permute-start | bytes 98312 | tf_op jit(solution)/shard_map/ppermute | solution.py:253
  25.0 5.0 %collective-permute-start.10 = (bf16[16,1024]{1,0:T(8,128)(2,1)S(1)}, bf16[16,1024]{1,0:T(8,128)(2,1)S(1)}, u32[]{:S(2)}, u32[]{:S(2)}) collective-permute-start(bf16[16,1024]{1,0:T(8,128)(2,1)S(1)} %get-tuple-element.23), channel_id=1, source_target_pairs={{0,4},{1,9},{2,6},{3,11},{4,0},{5,13},{6,2},{7,15},{8,12},{9,1},{1... | collective-permute-start | bytes 98312 | tf_op jit(solution)/shard_map/ppermute | solution.py:253
where the time goes:
time: 30.9 us; the launch traced here: 30.7 us
  starting transfers between devices  19.1 us (62%)
  waiting for transfers between devices  7.3 us (24%)
  Pallas kernels  3.51 us (11%)
  between operations  0.7 us (2%)
    ppermute x12, starting transfers between devices, turn_seq(): lax.ppermute(array, 'seq', [(place, target(place)) for place in range(seq...  12.4 us
    ppermute x12, waiting for transfers between devices, turn_seq(): lax.ppermute(array, 'seq', [(place, target(place)) for place in range(seq...  5.56 us
    ppermute x3, starting transfers between devices, across(): return lax.ppermute(array, 'kv', [(0, 1), (1, 0)])  4.66 us
    ppermute x1, starting transfers between devices, diagonal(): return lax.ppermute(array, ('kv', 'seq'), steps)  2.08 us
    ppermute x1, waiting for transfers between devices, diagonal(): return lax.ppermute(array, ('kv', 'seq'), steps)  1.73 us
    pallas_call x1, Pallas kernels, attend(): pl.pallas_call(functools.partial(attend_kernel, heads, groups, score_scal...  1.59 us
    pallas_call x1, Pallas kernels, pack(): pl.pallas_call(functools.partial(pack_kernel, heads, groups, score_scale)...  1.19 us
    pallas_call x1, Pallas kernels, finish(): pl.pallas_call(functools.partial(finish_kernel, groups, len(query_terms))...  0.73 us
  transfers between devices with their start and end apart: 16, of which 5 were waited for; matrix products, arithmetic and copies ran while one was open for 0% of the time, Pallas kernels for 0%

commit v1 on v0

--- a/solution.py
+++ b/solution.py
@@ -295,11 +295,14 @@
     order = ((0, 0), (2, 0), (3, 1), (4, 0), (1, 0), (3, 0), (2, 1), (5, 0))
     kinds = [jnp.float32] + [jnp.bfloat16] * 3
     dq_own, dq_other, *dpairs = attend(rows, order, pairs, [], kinds, heads, groups, score_scale)
-    parts = dpairs[1:]
-    pair_terms = [dpairs[0]] + [send(parts[place]) for send, place in ((middle, 0), (across, 1), (diagonal, 2))]
-    dq = (dq_own + f32(other_core(dq_other))).reshape(-1, own_rows, width)
-    query_terms = [dq[0]] + [
-        steps(bf16(dq[place]), even, odd) for place, even, odd in ((1, 1, 2), (2, 2, 1), (3, 3, 3))
+    arrived = other_core(dq_other)
+    dq = (dq_own + f32(arrived)).reshape(-1, own_rows, width)
+    dq, dpairs[3] = lax.optimization_barrier((dq, dpairs[3]))
+    pair_terms = [dpairs[0], middle(dpairs[1]), across(dpairs[2]), diagonal(dpairs[3])]
+    returned = [bf16(dq[place]) for place in range(4)]
+    returned[1], pair_terms[2] = lax.optimization_barrier((returned[1], pair_terms[2]))
+    query_terms = [
+        dq[0], steps(returned[1], 1, 2), steps(returned[2], 2, 1), steps(returned[3], 3, 3)
     ]
     return finish(query_terms, pair_terms, groups)
 
@@ -424,6 +427,7 @@
         kv_count == 2
         and seq_count == 16
         and queries.shape[0] % 16 == 0
+        and queries.shape[0] < LANES
         and video_keys.shape[0] % 16 == 0
         and video_keys.shape[1] == LANES
         and 2 * PIECES * saved_lse.shape[1] <= LANES

time: 30.9 us -> 30 us (0.971)
  waiting for transfers between devices: 7.3 us -> 6.35 us
    ppermute x1, waiting for transfers between devices: 1.73 us -> 0.09 us  [diagonal(): return lax.ppermute(array, ('kv', 'seq'), steps)]
    ppermute x12, waiting for transfers between devices: 5.56 us -> 6.25 us  [turn_seq(): lax.ppermute(array, 'seq', [(place, target(place)) for place in range(seq...]
    ppermute x12, starting transfers between devices: 12.4 us -> 13 us  [turn_seq(): lax.ppermute(array, 'seq', [(place, target(place)) for place in range(seq...]
    ppermute x3, starting transfers between devices: 4.66 us -> 4.3 us  [across(): return lax.ppermute(array, 'kv', [(0, 1), (1, 0)])]
  transfers between devices with their start and end apart: 16 -> 16, of which waited for: 5 -> 6; matrix products, arithmetic and copies ran while one was open for 0% -> 0% of each run, Pallas kernels for 0% -> 0%
where the time goes in v1:
time: 30 us; the launch traced here: 29.8 us
  starting transfers between devices  19.1 us (64%)
  waiting for transfers between devices  6.35 us (21%)
  Pallas kernels  3.51 us (12%)
  between operations  0.72 us (2%)
    ppermute x12, starting transfers between devices, turn_seq(): lax.ppermute(array, 'seq', [(place, target(place)) for place in range(seq...  13 us
    ppermute x12, waiting for transfers between devices, turn_seq(): lax.ppermute(array, 'seq', [(place, target(place)) for place in range(seq...  6.25 us
    ppermute x3, starting transfers between devices, across(): return lax.ppermute(array, 'kv', [(0, 1), (1, 0)])  4.3 us
    ppermute x1, starting transfers between devices, diagonal(): return lax.ppermute(array, ('kv', 'seq'), steps)  1.85 us
    pallas_call x1, Pallas kernels, attend(): pl.pallas_call(functools.partial(attend_kernel, heads, groups, score_scal...  1.59 us
    pallas_call x1, Pallas kernels, pack(): pl.pallas_call(functools.partial(pack_kernel, heads, groups, score_scale)...  1.19 us
    pallas_call x1, Pallas kernels, finish(): pl.pallas_call(functools.partial(finish_kernel, groups, len(query_terms))...  0.73 us
  transfers between devices with their start and end apart: 16, of which 6 were waited for; matrix products, arithmetic and copies ran while one was open for 0% of the time, Pallas kernels for 0%

profile of v1, /device:TPU:0, one launch (start us, length us, event | category | flops | bytes accessed | tf_op | source)
XLA Modules:
  0.0 29.8 jit_solution(2843852530908825484)
XLA Ops:
  0.6 1.2 %shard_map.85 = (bf16[16,2176]{1,0:T(8,128)(2,1)S(1)}, bf16[256,256]{1,0:T(8,128)(2,1)S(1)}) custom-call(bf16[16,1024]{1,0:T(8,128)(2,1)} %queries.1, bf16[16,1024]{1,0:T(8,128)(2,1)} %out_grad.1, bf16[16,1024]{1,0:T(8,128)(2,1)} %saved_out.1, f32[8,16]{1,0:T(8,128)} %bitcast.12, bf16[256,128]{1,0:T(8,128)(2,1)} %keys.1, bf16[256,128]{1,0:T(8,128)(2,1)} %values.1), custom_call_target="tpu_custom_call" | custom-call | tf_op jit(solution)/shard_map/pallas_call | solution.py:86
  1.8 0.5 %collective-permute-start = (bf16[16,2176]{1,0:T(8,128)(2,1)S(1)}, bf16[16,2176]{1,0:T(8,128)(2,1)S(1)}, u32[]{:S(2)}, u32[]{:S(2)}) collective-permute-start(bf16[16,2176]{1,0:T(8,128)(2,1)S(1)} %get-tuple-element.15.refs_0_), channel_id=1, source_target_pairs={{0,1},{1,0},{2,3},{3,2},{4,5},{5,4},{6,7},{7,6},{8,9},{9,8},{10,11... | collective-permute-start | bytes 208904 | tf_op jit(solution)/shard_map/ppermute | solution.py:253
  2.4 2.6 %collective-permute-start.6 = (bf16[256,256]{1,0:T(8,128)(2,1)S(1)}, bf16[256,256]{1,0:T(8,128)(2,1)S(1)}, u32[]{:S(2)}, u32[]{:S(2)}) collective-permute-start(bf16[256,256]{1,0:T(8,128)(2,1)S(1)} %get-tuple-element.16.refs_6_), channel_id=1, source_target_pairs={{0,16},{16,0},{1,17},{17,1},{2,18},{18,2},{3,19},{19,3},{4,20},{20... | collective-permute-start | bytes 393224 | tf_op jit(solution)/shard_map/ppermute | solution.py:274
  4.9 1.5 %collective-permute-start.5 = (bf16[256,256]{1,0:T(8,128)(2,1)S(1)}, bf16[256,256]{1,0:T(8,128)(2,1)S(1)}, u32[]{:S(2)}, u32[]{:S(2)}) collective-permute-start(bf16[256,256]{1,0:T(8,128)(2,1)S(1)} %get-tuple-element.16.refs_6_), channel_id=1, source_target_pairs={{0,2},{1,3},{2,0},{3,1},{4,6},{5,7},{6,4},{7,5},{8,10},{9,11},{10,... | collective-permute-start | bytes 393224 | tf_op jit(solution)/shard_map/ppermute | solution.py:253
  6.4 0.0 collective-permute-done.refs_1_
  6.5 1.6 %collective-permute-start.1 = (bf16[32,2176]{1,0:T(8,128)(2,1)S(1)}, bf16[32,2176]{1,0:T(8,128)(2,1)S(1)}, u32[]{:S(2)}, u32[]{:S(2)}) collective-permute-start(bf16[32,2176]{1,0:T(8,128)(2,1)S(1)} %pad_maximum_fusion), channel_id=1, source_target_pairs={{0,4},{1,9},{2,6},{3,11},{4,0},{5,13},{6,2},{7,15},{8,12},{9,1},{1... | collective-permute-start | bytes 417800 | tf_op jit(solution)/shard_map/ppermute | solution.py:253
  8.1 2.5 %collective-permute-start.3 = (bf16[16,2176]{1,0:T(8,128)(2,1)S(1)}, bf16[16,2176]{1,0:T(8,128)(2,1)S(1)}, u32[]{:S(2)}, u32[]{:S(2)}) collective-permute-start(bf16[16,2176]{1,0:T(8,128)(2,1)S(1)} %get-tuple-element.15.refs_0_), channel_id=1, source_target_pairs={{0,12},{1,13},{2,14},{3,15},{4,8},{5,9},{6,10},{7,11},{8,4},{9,5},... | collective-permute-start | bytes 208904 | tf_op jit(solution)/shard_map/ppermute | solution.py:253
  10.6 0.0 collective-permute-done.6.refs_8_
  10.6 0.6 %collective-permute-start.7 = (bf16[256,128]{1,0:T(8,128)(2,1)S(1)}, bf16[256,128]{1,0:T(8,128)(2,1)S(1)}, u32[]{:S(2)}, u32[]{:S(2)}) collective-permute-start(bf16[256,128]{1,0:T(8,128)(2,1)S(1)} %slice.27), channel_id=1, source_target_pairs={{0,2},{1,3},{2,0},{3,1},{4,6},{5,7},{6,4},{7,5},{8,10},{9,11},{10,... | collective-permute-start | bytes 196616 | tf_op jit(solution)/shard_map/ppermute | solution.py:253
  11.2 0.0 collective-permute-done.5.refs_7_
  11.2 1.2 %collective-permute-start.8 = (bf16[256,128]{1,0:T(8,128)(2,1)S(1)}, bf16[256,128]{1,0:T(8,128)(2,1)S(1)}, u32[]{:S(2)}, u32[]{:S(2)}) collective-permute-start(bf16[256,128]{1,0:T(8,128)(2,1)S(1)} %slice.28), channel_id=1, source_target_pairs={{0,16},{16,0},{1,17},{17,1},{2,18},{18,2},{3,19},{19,3},{4,20},{20... | collective-permute-start | bytes 196616 | tf_op jit(solution)/shard_map/ppermute | solution.py:274
  12.4 0.3 collective-permute-done.1.refs_2_
  12.6 0.5 %collective-permute-start.2 = (bf16[32,2176]{1,0:T(8,128)(2,1)S(1)}, bf16[32,2176]{1,0:T(8,128)(2,1)S(1)}, u32[]{:S(2)}, u32[]{:S(2)}) collective-permute-start(bf16[32,2176]{1,0:T(8,128)(2,1)S(1)} %collective-permute-done.1.refs_2_), channel_id=1, source_target_pairs={{0,1},{1,0},{2,3},{3,2},{4,5},{5,4},{6,7},{7,6},{8,9},{9,8},{10,11... | collective-permute-start | bytes 417800 | tf_op jit(solution)/shard_map/ppermute | solution.py:253
  13.1 2.4 %collective-permute-done.3.refs_4_ = bf16[16,2176]{1,0:T(8,128)(2,1)S(1)} collective-permute-done((bf16[16,2176]{1,0:T(8,128)(2,1)S(1)}, bf16[16,2176]{1,0:T(8,128)(2,1)S(1)}, u32[]{:S(2)}, u32[]{:S(2)}) %collective-permute-start.3) | collective-permute-done | bytes 69664 | tf_op jit(solution)/shard_map/ppermute | solution.py:253
  15.5 0.0 collective-permute-start.4
  15.5 0.0 collective-permute-done.7
  15.5 0.0 collective-permute-done.8
  15.5 1.2 %collective-permute-done.4.refs_5_ = bf16[16,2176]{1,0:T(8,128)(2,1)S(1)} collective-permute-done((bf16[16,2176]{1,0:T(8,128)(2,1)S(1)}, bf16[16,2176]{1,0:T(8,128)(2,1)S(1)}, u32[]{:S(2)}, u32[]{:S(2)}) %collective-permute-start.4) | collective-permute-done | bytes 69664 | tf_op jit(solution)/shard_map/ppermute | solution.py:253
  16.7 0.0 collective-permute-done.2.refs_3_
  16.8 1.6 %shard_map.86 = (f32[64,1024]{1,0:T(8,128)S(1)}, bf16[64,1024]{1,0:T(8,128)(2,1)S(1)}, f32[256,256]{1,0:T(8,128)S(1)}, bf16[256,256]{1,0:T(8,128)(2,1)S(1)}, bf1...) custom-call(bf16[16,2176]{1,0:T(8,128)(2,1)S(1)} %get-tuple-element.15.refs_0_, ...), custom_call_target="tpu_custom_call" | custom-call | flops 671088640 | tf_op jit(solution)/shard_map/pallas_call | solution.py:192
  18.4 0.2 collective-permute-start.9
  18.6 0.5 %collective-permute-start.10 = (bf16[256,256]{1,0:T(8,128)(2,1)S(1)}, bf16[256,256]{1,0:T(8,128)(2,1)S(1)}, u32[]{:S(2)}, u32[]{:S(2)}) collective-permute-start(bf16[256,256]{1,0:T(8,128)(2,1)S(1)} %get-tuple-element.21), channel_id=1, source_target_pairs={{0,16},{16,0},{1,17},{17,1},{2,18},{18,2},{3,19},{19,3},{4,20},{20... | collective-permute-start | bytes 393224 | tf_op jit(solution)/shard_map/ppermute | solution.py:274
  19.1 0.9 %collective-permute-start.14 = (bf16[256,256]{1,0:T(8,128)(2,1)S(1)}, bf16[256,256]{1,0:T(8,128)(2,1)S(1)}, u32[]{:S(2)}, u32[]{:S(2)}) collective-permute-start(bf16[256,256]{1,0:T(8,128)(2,1)S(1)} %get-tuple-element.24), channel_id=1, source_target_pairs={{0,2},{1,3},{2,0},{3,1},{4,6},{5,7},{6,4},{7,5},{8,10},{9,11},{10,... | collective-permute-start | bytes 393224 | tf_op jit(solution)/shard_map/ppermute | solution.py:253
  20.0 0.0 collective-permute-done.9
  20.1 3.1 %collective-permute-start.13 = (bf16[16,1024]{1,0:T(8,128)(2,1)S(1)}, bf16[16,1024]{1,0:T(8,128)(2,1)S(1)}, u32[]{:S(2)}, u32[]{:S(2)}) collective-permute-start(bf16[16,1024]{1,0:T(8,128)(2,1)S(1)} %get-tuple-element.27), channel_id=1, source_target_pairs={{0,12},{1,13},{2,14},{3,15},{4,8},{5,9},{6,10},{7,11},{8,4},{9,5},... | collective-permute-start | bytes 98312 | tf_op jit(solution)/shard_map/ppermute | solution.py:253
  23.2 0.0 collective-permute-start.12
  23.2 1.9 %collective-permute-start.15 = (bf16[256,256]{1,0:T(8,128)(2,1)S(1)}, bf16[256,256]{1,0:T(8,128)(2,1)S(1)}, u32[]{:S(2)}, u32[]{:S(2)}) collective-permute-start(bf16[256,256]{1,0:T(8,128)(2,1)S(1)} %get-tuple-element.26), channel_id=1, source_target_pairs={{0,18},{1,19},{2,16},{3,17},{4,22},{5,23},{6,20},{7,21},{8,26},{9,... | collective-permute-start | bytes 393224 | tf_op jit(solution)/shard_map/ppermute | solution.py:282
  25.1 0.0 collective-permute-done.10.refs_6_
  25.1 1.5 %collective-permute-start.11 = (bf16[16,1024]{1,0:T(8,128)(2,1)S(1)}, bf16[16,1024]{1,0:T(8,128)(2,1)S(1)}, u32[]{:S(2)}, u32[]{:S(2)}) collective-permute-start(bf16[16,1024]{1,0:T(8,128)(2,1)S(1)} %get-tuple-element.22), channel_id=1, source_target_pairs={{0,4},{1,9},{2,6},{3,11},{4,0},{5,13},{6,2},{7,15},{8,12},{9,1},{1... | collective-permute-start | bytes 98312 | tf_op jit(solution)/shard_map/ppermute | solution.py:253
  26.6 0.0 collective-permute-done.14.refs_5_
  26.6 0.0 collective-permute-done.13.refs_3_
  26.6 1.8 %collective-permute-done.12.refs_2_ = bf16[16,1024]{1,0:T(8,128)(2,1)S(1)} collective-permute-done((bf16[16,1024]{1,0:T(8,128)(2,1)S(1)}, bf16[16,1024]{1,0:T(8,128)(2,1)S(1)}, u32[]{:S(2)}, u32[]{:S(2)}) %collective-permute-start.12) | collective-permute-done | bytes 32800 | tf_op jit(solution)/shard_map/ppermute | solution.py:253
  28.4 0.6 %collective-permute-done.11.refs_1_ = bf16[16,1024]{1,0:T(8,128)(2,1)S(1)} collective-permute-done((bf16[16,1024]{1,0:T(8,128)(2,1)S(1)}, bf16[16,1024]{1,0:T(8,128)(2,1)S(1)}, u32[]{:S(2)}, u32[]{:S(2)}) %collective-permute-start.11) | collective-permute-done | bytes 32800 | tf_op jit(solution)/shard_map/ppermute | solution.py:253
  29.0 0.1 collective-permute-done.15.refs_7_
  29.1 0.7 %shard_map.87 = (bf16[16,1024]{1,0:T(8,128)(2,1)}, bf16[256,128]{1,0:T(8,128)(2,1)}, bf16[256,128]{1,0:T(8,128)(2,1)}) custom-call(f32[16,1024]{1,0:T(8,128)S(1)} %slice_bitcast_fusion.refs_0_, bf16[16,1024]{1,0:T(8,128)(2,1)S(1)} %collective-permute-done.11.refs_1_, bf16[16,1024]{1,0:T(8,128)(2,1)S(1)} %collective-permute-done.12.refs_2_, ...), custom_call_target="tpu_custom_call" | custom-call | tf_op jit(solution)/shard_map/pallas_call | solution.py:241
  (8 shorter events, 0.1 us)
Async XLA Ops:
  1.8 4.6 %collective-permute-start = (bf16[16,2176]{1,0:T(8,128)(2,1)S(1)}, bf16[16,2176]{1,0:T(8,128)(2,1)S(1)}, u32[]{:S(2)}, u32[]{:S(2)}) collective-permute-start(bf16[16,2176]{1,0:T(8,128)(2,1)S(1)} %get-tuple-element.15.refs_0_), channel_id=1, source_target_pairs={{0,1},{1,0},{2,3},{3,2},{4,5},{5,4},{6,7},{7,6},{8,9},{9,8},{10,11... | collective-permute-start | bytes 208904 | tf_op jit(solution)/shard_map/ppermute | solution.py:253
  2.4 8.2 %collective-permute-start.6 = (bf16[256,256]{1,0:T(8,128)(2,1)S(1)}, bf16[256,256]{1,0:T(8,128)(2,1)S(1)}, u32[]{:S(2)}, u32[]{:S(2)}) collective-permute-start(bf16[256,256]{1,0:T(8,128)(2,1)S(1)} %get-tuple-element.16.refs_6_), channel_id=1, source_target_pairs={{0,16},{16,0},{1,17},{17,1},{2,18},{18,2},{3,19},{19,3},{4,20},{20... | collective-permute-start | bytes 393224 | tf_op jit(solution)/shard_map/ppermute | solution.py:274
  4.9 6.2 %collective-permute-start.5 = (bf16[256,256]{1,0:T(8,128)(2,1)S(1)}, bf16[256,256]{1,0:T(8,128)(2,1)S(1)}, u32[]{:S(2)}, u32[]{:S(2)}) collective-permute-start(bf16[256,256]{1,0:T(8,128)(2,1)S(1)} %get-tuple-element.16.refs_6_), channel_id=1, source_target_pairs={{0,2},{1,3},{2,0},{3,1},{4,6},{5,7},{6,4},{7,5},{8,10},{9,11},{10,... | collective-permute-start | bytes 393224 | tf_op jit(solution)/shard_map/ppermute | solution.py:253
  6.5 6.2 %collective-permute-start.1 = (bf16[32,2176]{1,0:T(8,128)(2,1)S(1)}, bf16[32,2176]{1,0:T(8,128)(2,1)S(1)}, u32[]{:S(2)}, u32[]{:S(2)}) collective-permute-start(bf16[32,2176]{1,0:T(8,128)(2,1)S(1)} %pad_maximum_fusion), channel_id=1, source_target_pairs={{0,4},{1,9},{2,6},{3,11},{4,0},{5,13},{6,2},{7,15},{8,12},{9,1},{1... | collective-permute-start | bytes 417800 | tf_op jit(solution)/shard_map/ppermute | solution.py:253
  8.1 7.4 %collective-permute-start.3 = (bf16[16,2176]{1,0:T(8,128)(2,1)S(1)}, bf16[16,2176]{1,0:T(8,128)(2,1)S(1)}, u32[]{:S(2)}, u32[]{:S(2)}) collective-permute-start(bf16[16,2176]{1,0:T(8,128)(2,1)S(1)} %get-tuple-element.15.refs_0_), channel_id=1, source_target_pairs={{0,12},{1,13},{2,14},{3,15},{4,8},{5,9},{6,10},{7,11},{8,4},{9,5},... | collective-permute-start | bytes 208904 | tf_op jit(solution)/shard_map/ppermute | solution.py:253
  10.6 4.9 %collective-permute-start.7 = (bf16[256,128]{1,0:T(8,128)(2,1)S(1)}, bf16[256,128]{1,0:T(8,128)(2,1)S(1)}, u32[]{:S(2)}, u32[]{:S(2)}) collective-permute-start(bf16[256,128]{1,0:T(8,128)(2,1)S(1)} %slice.27), channel_id=1, source_target_pairs={{0,2},{1,3},{2,0},{3,1},{4,6},{5,7},{6,4},{7,5},{8,10},{9,11},{10,... | collective-permute-start | bytes 196616 | tf_op jit(solution)/shard_map/ppermute | solution.py:253
  11.2 4.3 %collective-permute-start.8 = (bf16[256,128]{1,0:T(8,128)(2,1)S(1)}, bf16[256,128]{1,0:T(8,128)(2,1)S(1)}, u32[]{:S(2)}, u32[]{:S(2)}) collective-permute-start(bf16[256,128]{1,0:T(8,128)(2,1)S(1)} %slice.28), channel_id=1, source_target_pairs={{0,16},{16,0},{1,17},{17,1},{2,18},{18,2},{3,19},{19,3},{4,20},{20... | collective-permute-start | bytes 196616 | tf_op jit(solution)/shard_map/ppermute | solution.py:274
  12.6 4.1 %collective-permute-start.2 = (bf16[32,2176]{1,0:T(8,128)(2,1)S(1)}, bf16[32,2176]{1,0:T(8,128)(2,1)S(1)}, u32[]{:S(2)}, u32[]{:S(2)}) collective-permute-start(bf16[32,2176]{1,0:T(8,128)(2,1)S(1)} %collective-permute-done.1.refs_2_), channel_id=1, source_target_pairs={{0,1},{1,0},{2,3},{3,2},{4,5},{5,4},{6,7},{7,6},{8,9},{9,8},{10,11... | collective-permute-start | bytes 417800 | tf_op jit(solution)/shard_map/ppermute | solution.py:253
  15.5 1.3 %collective-permute-start.4 = (bf16[16,2176]{1,0:T(8,128)(2,1)S(1)}, bf16[16,2176]{1,0:T(8,128)(2,1)S(1)}, u32[]{:S(2)}, u32[]{:S(2)}) collective-permute-start(bf16[16,2176]{1,0:T(8,128)(2,1)S(1)} %collective-permute-done.3.refs_4_), channel_id=1, source_target_pairs={{0,1},{1,0},{2,3},{3,2},{4,5},{5,4},{6,7},{7,6},{8,9},{9,8},{10,11... | collective-permute-start | bytes 208904 | tf_op jit(solution)/shard_map/ppermute | solution.py:253
  18.4 1.6 %collective-permute-start.9 = (bf16[64,1024]{1,0:T(8,128)(2,1)S(1)}, bf16[64,1024]{1,0:T(8,128)(2,1)S(1)}, u32[]{:S(2)}, u32[]{:S(2)}) collective-permute-start(bf16[64,1024]{1,0:T(8,128)(2,1)S(1)} %get-tuple-element.18), channel_id=1, source_target_pairs={{0,1},{1,0},{2,3},{3,2},{4,5},{5,4},{6,7},{7,6},{8,9},{9,8},{10,11... | collective-permute-start | bytes 393224 | tf_op jit(solution)/shard_map/ppermute | solution.py:253
  18.6 6.5 %collective-permute-start.10 = (bf16[256,256]{1,0:T(8,128)(2,1)S(1)}, bf16[256,256]{1,0:T(8,128)(2,1)S(1)}, u32[]{:S(2)}, u32[]{:S(2)}) collective-permute-start(bf16[256,256]{1,0:T(8,128)(2,1)S(1)} %get-tuple-element.21), channel_id=1, source_target_pairs={{0,16},{16,0},{1,17},{17,1},{2,18},{18,2},{3,19},{19,3},{4,20},{20... | collective-permute-start | bytes 393224 | tf_op jit(solution)/shard_map/ppermute | solution.py:274
  19.1 7.5 %collective-permute-start.14 = (bf16[256,256]{1,0:T(8,128)(2,1)S(1)}, bf16[256,256]{1,0:T(8,128)(2,1)S(1)}, u32[]{:S(2)}, u32[]{:S(2)}) collective-permute-start(bf16[256,256]{1,0:T(8,128)(2,1)S(1)} %get-tuple-element.24), channel_id=1, source_target_pairs={{0,2},{1,3},{2,0},{3,1},{4,6},{5,7},{6,4},{7,5},{8,10},{9,11},{10,... | collective-permute-start | bytes 393224 | tf_op jit(solution)/shard_map/ppermute | solution.py:253
  20.1 6.6 %collective-permute-start.13 = (bf16[16,1024]{1,0:T(8,128)(2,1)S(1)}, bf16[16,1024]{1,0:T(8,128)(2,1)S(1)}, u32[]{:S(2)}, u32[]{:S(2)}) collective-permute-start(bf16[16,1024]{1,0:T(8,128)(2,1)S(1)} %get-tuple-element.27), channel_id=1, source_target_pairs={{0,12},{1,13},{2,14},{3,15},{4,8},{5,9},{6,10},{7,11},{8,4},{9,5},... | collective-permute-start | bytes 98312 | tf_op jit(solution)/shard_map/ppermute | solution.py:253
  23.2 5.2 %collective-permute-start.12 = (bf16[16,1024]{1,0:T(8,128)(2,1)S(1)}, bf16[16,1024]{1,0:T(8,128)(2,1)S(1)}, u32[]{:S(2)}, u32[]{:S(2)}) collective-permute-start(bf16[16,1024]{1,0:T(8,128)(2,1)S(1)} %get-tuple-element.28), channel_id=1, source_target_pairs={{0,8},{1,5},{2,10},{3,7},{4,12},{5,1},{6,14},{7,3},{8,0},{9,13},{1... | collective-permute-start | bytes 98312 | tf_op jit(solution)/shard_map/ppermute | solution.py:253
  23.2 5.9 %collective-permute-start.15 = (bf16[256,256]{1,0:T(8,128)(2,1)S(1)}, bf16[256,256]{1,0:T(8,128)(2,1)S(1)}, u32[]{:S(2)}, u32[]{:S(2)}) collective-permute-start(bf16[256,256]{1,0:T(8,128)(2,1)S(1)} %get-tuple-element.26), channel_id=1, source_target_pairs={{0,18},{1,19},{2,16},{3,17},{4,22},{5,23},{6,20},{7,21},{8,26},{9,... | collective-permute-start | bytes 393224 | tf_op jit(solution)/shard_map/ppermute | solution.py:282
  25.1 3.9 %collective-permute-start.11 = (bf16[16,1024]{1,0:T(8,128)(2,1)S(1)}, bf16[16,1024]{1,0:T(8,128)(2,1)S(1)}, u32[]{:S(2)}, u32[]{:S(2)}) collective-permute-start(bf16[16,1024]{1,0:T(8,128)(2,1)S(1)} %get-tuple-element.22), channel_id=1, source_target_pairs={{0,4},{1,9},{2,6},{3,11},{4,0},{5,13},{6,2},{7,15},{8,12},{9,1},{1... | collective-permute-start | bytes 98312 | tf_op jit(solution)/shard_map/ppermute | solution.py:253

commit v2 on v1

--- a/solution.py
+++ b/solution.py
@@ -285,8 +285,8 @@
         queries, out_grad, saved_out, saved_lse.T, video_keys, video_values, groups, score_scale
     )
     pair_across, pair_middle = across(pair), middle(pair)
-    keys_far = middle(pair_across[:, :head_width])
-    values_far = across(pair_middle[:, head_width:])
+    values_far = middle(pair_across[:, head_width:])
+    keys_far = across(pair_middle[:, :head_width])
     pairs = [pair, pair_middle, pair_across, jnp.concatenate([keys_far, values_far], axis=1)]
     beside = other_core(packed)
     from_far = steps(packed, 3, 3)

time: 30 us -> 30 us (level)
  no operation moved by 1% of the time
where the time goes in v2:
time: 30 us; the launch traced here: 29.8 us
  starting transfers between devices  19.1 us (64%)
  waiting for transfers between devices  6.35 us (21%)
  Pallas kernels  3.51 us (12%)
  between operations  0.72 us (2%)
    ppermute x12, starting transfers between devices, turn_seq(): lax.ppermute(array, 'seq', [(place, target(place)) for place in range(seq...  13 us
    ppermute x12, waiting for transfers between devices, turn_seq(): lax.ppermute(array, 'seq', [(place, target(place)) for place in range(seq...  6.25 us
    ppermute x3, starting transfers between devices, across(): return lax.ppermute(array, 'kv', [(0, 1), (1, 0)])  4.3 us
    ppermute x1, starting transfers between devices, diagonal(): return lax.ppermute(array, ('kv', 'seq'), steps)  1.85 us
    pallas_call x1, Pallas kernels, attend(): pl.pallas_call(functools.partial(attend_kernel, heads, groups, score_scal...  1.59 us
    pallas_call x1, Pallas kernels, pack(): pl.pallas_call(functools.partial(pack_kernel, heads, groups, score_scale)...  1.19 us
    pallas_call x1, Pallas kernels, finish(): pl.pallas_call(functools.partial(finish_kernel, groups, len(query_terms))...  0.73 us
  transfers between devices with their start and end apart: 16, of which 6 were waited for; matrix products, arithmetic and copies ran while one was open for 0% of the time, Pallas kernels for 0%

profile of v2, /device:TPU:0, one launch (start us, length us, event | category | flops | bytes accessed | tf_op | source)
XLA Modules:
  0.0 29.8 jit_solution(14488879710953461149)
XLA Ops:
  0.6 1.2 %shard_map.85 = (bf16[16,2176]{1,0:T(8,128)(2,1)S(1)}, bf16[256,256]{1,0:T(8,128)(2,1)S(1)}) custom-call(bf16[16,1024]{1,0:T(8,128)(2,1)} %queries.1, bf16[16,1024]{1,0:T(8,128)(2,1)} %out_grad.1, bf16[16,1024]{1,0:T(8,128)(2,1)} %saved_out.1, f32[8,16]{1,0:T(8,128)} %bitcast.12, bf16[256,128]{1,0:T(8,128)(2,1)} %keys.1, bf16[256,128]{1,0:T(8,128)(2,1)} %values.1), custom_call_target="tpu_custom_call" | custom-call | tf_op jit(solution)/shard_map/pallas_call | solution.py:86
  1.8 0.5 %collective-permute-start = (bf16[16,2176]{1,0:T(8,128)(2,1)S(1)}, bf16[16,2176]{1,0:T(8,128)(2,1)S(1)}, u32[]{:S(2)}, u32[]{:S(2)}) collective-permute-start(bf16[16,2176]{1,0:T(8,128)(2,1)S(1)} %get-tuple-element.15.refs_0_), channel_id=1, source_target_pairs={{0,1},{1,0},{2,3},{3,2},{4,5},{5,4},{6,7},{7,6},{8,9},{9,8},{10,11... | collective-permute-start | bytes 208904 | tf_op jit(solution)/shard_map/ppermute | solution.py:253
  2.4 2.6 %collective-permute-start.6 = (bf16[256,256]{1,0:T(8,128)(2,1)S(1)}, bf16[256,256]{1,0:T(8,128)(2,1)S(1)}, u32[]{:S(2)}, u32[]{:S(2)}) collective-permute-start(bf16[256,256]{1,0:T(8,128)(2,1)S(1)} %get-tuple-element.16.refs_6_), channel_id=1, source_target_pairs={{0,16},{16,0},{1,17},{17,1},{2,18},{18,2},{3,19},{19,3},{4,20},{20... | collective-permute-start | bytes 393224 | tf_op jit(solution)/shard_map/ppermute | solution.py:274
  4.9 1.5 %collective-permute-start.5 = (bf16[256,256]{1,0:T(8,128)(2,1)S(1)}, bf16[256,256]{1,0:T(8,128)(2,1)S(1)}, u32[]{:S(2)}, u32[]{:S(2)}) collective-permute-start(bf16[256,256]{1,0:T(8,128)(2,1)S(1)} %get-tuple-element.16.refs_6_), channel_id=1, source_target_pairs={{0,2},{1,3},{2,0},{3,1},{4,6},{5,7},{6,4},{7,5},{8,10},{9,11},{10,... | collective-permute-start | bytes 393224 | tf_op jit(solution)/shard_map/ppermute | solution.py:253
  6.4 0.0 collective-permute-done.refs_1_
  6.5 1.6 %collective-permute-start.1 = (bf16[32,2176]{1,0:T(8,128)(2,1)S(1)}, bf16[32,2176]{1,0:T(8,128)(2,1)S(1)}, u32[]{:S(2)}, u32[]{:S(2)}) collective-permute-start(bf16[32,2176]{1,0:T(8,128)(2,1)S(1)} %pad_maximum_fusion), channel_id=1, source_target_pairs={{0,4},{1,9},{2,6},{3,11},{4,0},{5,13},{6,2},{7,15},{8,12},{9,1},{1... | collective-permute-start | bytes 417800 | tf_op jit(solution)/shard_map/ppermute | solution.py:253
  8.1 2.5 %collective-permute-start.3 = (bf16[16,2176]{1,0:T(8,128)(2,1)S(1)}, bf16[16,2176]{1,0:T(8,128)(2,1)S(1)}, u32[]{:S(2)}, u32[]{:S(2)}) collective-permute-start(bf16[16,2176]{1,0:T(8,128)(2,1)S(1)} %get-tuple-element.15.refs_0_), channel_id=1, source_target_pairs={{0,12},{1,13},{2,14},{3,15},{4,8},{5,9},{6,10},{7,11},{8,4},{9,5},... | collective-permute-start | bytes 208904 | tf_op jit(solution)/shard_map/ppermute | solution.py:253
  10.6 0.0 collective-permute-done.6.refs_8_
  10.6 0.6 %collective-permute-start.8 = (bf16[256,128]{1,0:T(8,128)(2,1)S(1)}, bf16[256,128]{1,0:T(8,128)(2,1)S(1)}, u32[]{:S(2)}, u32[]{:S(2)}) collective-permute-start(bf16[256,128]{1,0:T(8,128)(2,1)S(1)} %slice.28), channel_id=1, source_target_pairs={{0,2},{1,3},{2,0},{3,1},{4,6},{5,7},{6,4},{7,5},{8,10},{9,11},{10,... | collective-permute-start | bytes 196616 | tf_op jit(solution)/shard_map/ppermute | solution.py:253
  11.2 0.0 collective-permute-done.5.refs_7_
  11.2 1.2 %collective-permute-start.7 = (bf16[256,128]{1,0:T(8,128)(2,1)S(1)}, bf16[256,128]{1,0:T(8,128)(2,1)S(1)}, u32[]{:S(2)}, u32[]{:S(2)}) collective-permute-start(bf16[256,128]{1,0:T(8,128)(2,1)S(1)} %slice.27), channel_id=1, source_target_pairs={{0,16},{16,0},{1,17},{17,1},{2,18},{18,2},{3,19},{19,3},{4,20},{20... | collective-permute-start | bytes 196616 | tf_op jit(solution)/shard_map/ppermute | solution.py:274
  12.4 0.3 collective-permute-done.1.refs_2_
  12.6 0.5 %collective-permute-start.2 = (bf16[32,2176]{1,0:T(8,128)(2,1)S(1)}, bf16[32,2176]{1,0:T(8,128)(2,1)S(1)}, u32[]{:S(2)}, u32[]{:S(2)}) collective-permute-start(bf16[32,2176]{1,0:T(8,128)(2,1)S(1)} %collective-permute-done.1.refs_2_), channel_id=1, source_target_pairs={{0,1},{1,0},{2,3},{3,2},{4,5},{5,4},{6,7},{7,6},{8,9},{9,8},{10,11... | collective-permute-start | bytes 417800 | tf_op jit(solution)/shard_map/ppermute | solution.py:253
  13.1 2.4 %collective-permute-done.3.refs_4_ = bf16[16,2176]{1,0:T(8,128)(2,1)S(1)} collective-permute-done((bf16[16,2176]{1,0:T(8,128)(2,1)S(1)}, bf16[16,2176]{1,0:T(8,128)(2,1)S(1)}, u32[]{:S(2)}, u32[]{:S(2)}) %collective-permute-start.3) | collective-permute-done | bytes 69664 | tf_op jit(solution)/shard_map/ppermute | solution.py:253
  15.5 0.0 collective-permute-start.4
  15.5 0.0 collective-permute-done.8
  15.5 0.0 collective-permute-done.7
  15.5 1.2 %collective-permute-done.4.refs_5_ = bf16[16,2176]{1,0:T(8,128)(2,1)S(1)} collective-permute-done((bf16[16,2176]{1,0:T(8,128)(2,1)S(1)}, bf16[16,2176]{1,0:T(8,128)(2,1)S(1)}, u32[]{:S(2)}, u32[]{:S(2)}) %collective-permute-start.4) | collective-permute-done | bytes 69664 | tf_op jit(solution)/shard_map/ppermute | solution.py:253
  16.7 0.0 collective-permute-done.2.refs_3_
  16.8 1.6 %shard_map.86 = (f32[64,1024]{1,0:T(8,128)S(1)}, bf16[64,1024]{1,0:T(8,128)(2,1)S(1)}, f32[256,256]{1,0:T(8,128)S(1)}, bf16[256,256]{1,0:T(8,128)(2,1)S(1)}, bf1...) custom-call(bf16[16,2176]{1,0:T(8,128)(2,1)S(1)} %get-tuple-element.15.refs_0_, ...), custom_call_target="tpu_custom_call" | custom-call | flops 671088640 | tf_op jit(solution)/shard_map/pallas_call | solution.py:192
  18.4 0.2 collective-permute-start.9
  18.6 0.5 %collective-permute-start.10 = (bf16[256,256]{1,0:T(8,128)(2,1)S(1)}, bf16[256,256]{1,0:T(8,128)(2,1)S(1)}, u32[]{:S(2)}, u32[]{:S(2)}) collective-permute-start(bf16[256,256]{1,0:T(8,128)(2,1)S(1)} %get-tuple-element.21), channel_id=1, source_target_pairs={{0,16},{16,0},{1,17},{17,1},{2,18},{18,2},{3,19},{19,3},{4,20},{20... | collective-permute-start | bytes 393224 | tf_op jit(solution)/shard_map/ppermute | solution.py:274
  19.1 0.9 %collective-permute-start.14 = (bf16[256,256]{1,0:T(8,128)(2,1)S(1)}, bf16[256,256]{1,0:T(8,128)(2,1)S(1)}, u32[]{:S(2)}, u32[]{:S(2)}) collective-permute-start(bf16[256,256]{1,0:T(8,128)(2,1)S(1)} %get-tuple-element.24), channel_id=1, source_target_pairs={{0,2},{1,3},{2,0},{3,1},{4,6},{5,7},{6,4},{7,5},{8,10},{9,11},{10,... | collective-permute-start | bytes 393224 | tf_op jit(solution)/shard_map/ppermute | solution.py:253
  20.0 0.0 collective-permute-done.9
  20.1 3.1 %collective-permute-start.13 = (bf16[16,1024]{1,0:T(8,128)(2,1)S(1)}, bf16[16,1024]{1,0:T(8,128)(2,1)S(1)}, u32[]{:S(2)}, u32[]{:S(2)}) collective-permute-start(bf16[16,1024]{1,0:T(8,128)(2,1)S(1)} %get-tuple-element.27), channel_id=1, source_target_pairs={{0,12},{1,13},{2,14},{3,15},{4,8},{5,9},{6,10},{7,11},{8,4},{9,5},... | collective-permute-start | bytes 98312 | tf_op jit(solution)/shard_map/ppermute | solution.py:253
  23.2 0.0 collective-permute-start.12
  23.2 1.9 %collective-permute-start.15 = (bf16[256,256]{1,0:T(8,128)(2,1)S(1)}, bf16[256,256]{1,0:T(8,128)(2,1)S(1)}, u32[]{:S(2)}, u32[]{:S(2)}) collective-permute-start(bf16[256,256]{1,0:T(8,128)(2,1)S(1)} %get-tuple-element.26), channel_id=1, source_target_pairs={{0,18},{1,19},{2,16},{3,17},{4,22},{5,23},{6,20},{7,21},{8,26},{9,... | collective-permute-start | bytes 393224 | tf_op jit(solution)/shard_map/ppermute | solution.py:282
  25.1 0.0 collective-permute-done.10.refs_6_
  25.1 1.5 %collective-permute-start.11 = (bf16[16,1024]{1,0:T(8,128)(2,1)S(1)}, bf16[16,1024]{1,0:T(8,128)(2,1)S(1)}, u32[]{:S(2)}, u32[]{:S(2)}) collective-permute-start(bf16[16,1024]{1,0:T(8,128)(2,1)S(1)} %get-tuple-element.22), channel_id=1, source_target_pairs={{0,4},{1,9},{2,6},{3,11},{4,0},{5,13},{6,2},{7,15},{8,12},{9,1},{1... | collective-permute-start | bytes 98312 | tf_op jit(solution)/shard_map/ppermute | solution.py:253
  26.6 0.0 collective-permute-done.14.refs_5_
  26.6 0.0 collective-permute-done.13.refs_3_
  26.6 1.8 %collective-permute-done.12.refs_2_ = bf16[16,1024]{1,0:T(8,128)(2,1)S(1)} collective-permute-done((bf16[16,1024]{1,0:T(8,128)(2,1)S(1)}, bf16[16,1024]{1,0:T(8,128)(2,1)S(1)}, u32[]{:S(2)}, u32[]{:S(2)}) %collective-permute-start.12) | collective-permute-done | bytes 32800 | tf_op jit(solution)/shard_map/ppermute | solution.py:253
  28.4 0.6 %collective-permute-done.11.refs_1_ = bf16[16,1024]{1,0:T(8,128)(2,1)S(1)} collective-permute-done((bf16[16,1024]{1,0:T(8,128)(2,1)S(1)}, bf16[16,1024]{1,0:T(8,128)(2,1)S(1)}, u32[]{:S(2)}, u32[]{:S(2)}) %collective-permute-start.11) | collective-permute-done | bytes 32800 | tf_op jit(solution)/shard_map/ppermute | solution.py:253
  29.0 0.1 collective-permute-done.15.refs_7_
  29.1 0.7 %shard_map.87 = (bf16[16,1024]{1,0:T(8,128)(2,1)}, bf16[256,128]{1,0:T(8,128)(2,1)}, bf16[256,128]{1,0:T(8,128)(2,1)}) custom-call(f32[16,1024]{1,0:T(8,128)S(1)} %slice_bitcast_fusion.refs_0_, bf16[16,1024]{1,0:T(8,128)(2,1)S(1)} %collective-permute-done.11.refs_1_, bf16[16,1024]{1,0:T(8,128)(2,1)S(1)} %collective-permute-done.12.refs_2_, ...), custom_call_target="tpu_custom_call" | custom-call | tf_op jit(solution)/shard_map/pallas_call | solution.py:241
  (8 shorter events, 0.1 us)
Async XLA Ops:
  1.8 4.6 %collective-permute-start = (bf16[16,2176]{1,0:T(8,128)(2,1)S(1)}, bf16[16,2176]{1,0:T(8,128)(2,1)S(1)}, u32[]{:S(2)}, u32[]{:S(2)}) collective-permute-start(bf16[16,2176]{1,0:T(8,128)(2,1)S(1)} %get-tuple-element.15.refs_0_), channel_id=1, source_target_pairs={{0,1},{1,0},{2,3},{3,2},{4,5},{5,4},{6,7},{7,6},{8,9},{9,8},{10,11... | collective-permute-start | bytes 208904 | tf_op jit(solution)/shard_map/ppermute | solution.py:253
  2.4 8.2 %collective-permute-start.6 = (bf16[256,256]{1,0:T(8,128)(2,1)S(1)}, bf16[256,256]{1,0:T(8,128)(2,1)S(1)}, u32[]{:S(2)}, u32[]{:S(2)}) collective-permute-start(bf16[256,256]{1,0:T(8,128)(2,1)S(1)} %get-tuple-element.16.refs_6_), channel_id=1, source_target_pairs={{0,16},{16,0},{1,17},{17,1},{2,18},{18,2},{3,19},{19,3},{4,20},{20... | collective-permute-start | bytes 393224 | tf_op jit(solution)/shard_map/ppermute | solution.py:274
  4.9 6.2 %collective-permute-start.5 = (bf16[256,256]{1,0:T(8,128)(2,1)S(1)}, bf16[256,256]{1,0:T(8,128)(2,1)S(1)}, u32[]{:S(2)}, u32[]{:S(2)}) collective-permute-start(bf16[256,256]{1,0:T(8,128)(2,1)S(1)} %get-tuple-element.16.refs_6_), channel_id=1, source_target_pairs={{0,2},{1,3},{2,0},{3,1},{4,6},{5,7},{6,4},{7,5},{8,10},{9,11},{10,... | collective-permute-start | bytes 393224 | tf_op jit(solution)/shard_map/ppermute | solution.py:253
  6.5 6.2 %collective-permute-start.1 = (bf16[32,2176]{1,0:T(8,128)(2,1)S(1)}, bf16[32,2176]{1,0:T(8,128)(2,1)S(1)}, u32[]{:S(2)}, u32[]{:S(2)}) collective-permute-start(bf16[32,2176]{1,0:T(8,128)(2,1)S(1)} %pad_maximum_fusion), channel_id=1, source_target_pairs={{0,4},{1,9},{2,6},{3,11},{4,0},{5,13},{6,2},{7,15},{8,12},{9,1},{1... | collective-permute-start | bytes 417800 | tf_op jit(solution)/shard_map/ppermute | solution.py:253
  8.1 7.4 %collective-permute-start.3 = (bf16[16,2176]{1,0:T(8,128)(2,1)S(1)}, bf16[16,2176]{1,0:T(8,128)(2,1)S(1)}, u32[]{:S(2)}, u32[]{:S(2)}) collective-permute-start(bf16[16,2176]{1,0:T(8,128)(2,1)S(1)} %get-tuple-element.15.refs_0_), channel_id=1, source_target_pairs={{0,12},{1,13},{2,14},{3,15},{4,8},{5,9},{6,10},{7,11},{8,4},{9,5},... | collective-permute-start | bytes 208904 | tf_op jit(solution)/shard_map/ppermute | solution.py:253
  10.6 4.9 %collective-permute-start.8 = (bf16[256,128]{1,0:T(8,128)(2,1)S(1)}, bf16[256,128]{1,0:T(8,128)(2,1)S(1)}, u32[]{:S(2)}, u32[]{:S(2)}) collective-permute-start(bf16[256,128]{1,0:T(8,128)(2,1)S(1)} %slice.28), channel_id=1, source_target_pairs={{0,2},{1,3},{2,0},{3,1},{4,6},{5,7},{6,4},{7,5},{8,10},{9,11},{10,... | collective-permute-start | bytes 196616 | tf_op jit(solution)/shard_map/ppermute | solution.py:253
  11.2 4.3 %collective-permute-start.7 = (bf16[256,128]{1,0:T(8,128)(2,1)S(1)}, bf16[256,128]{1,0:T(8,128)(2,1)S(1)}, u32[]{:S(2)}, u32[]{:S(2)}) collective-permute-start(bf16[256,128]{1,0:T(8,128)(2,1)S(1)} %slice.27), channel_id=1, source_target_pairs={{0,16},{16,0},{1,17},{17,1},{2,18},{18,2},{3,19},{19,3},{4,20},{20... | collective-permute-start | bytes 196616 | tf_op jit(solution)/shard_map/ppermute | solution.py:274
  12.6 4.1 %collective-permute-start.2 = (bf16[32,2176]{1,0:T(8,128)(2,1)S(1)}, bf16[32,2176]{1,0:T(8,128)(2,1)S(1)}, u32[]{:S(2)}, u32[]{:S(2)}) collective-permute-start(bf16[32,2176]{1,0:T(8,128)(2,1)S(1)} %collective-permute-done.1.refs_2_), channel_id=1, source_target_pairs={{0,1},{1,0},{2,3},{3,2},{4,5},{5,4},{6,7},{7,6},{8,9},{9,8},{10,11... | collective-permute-start | bytes 417800 | tf_op jit(solution)/shard_map/ppermute | solution.py:253
  15.5 1.3 %collective-permute-start.4 = (bf16[16,2176]{1,0:T(8,128)(2,1)S(1)}, bf16[16,2176]{1,0:T(8,128)(2,1)S(1)}, u32[]{:S(2)}, u32[]{:S(2)}) collective-permute-start(bf16[16,2176]{1,0:T(8,128)(2,1)S(1)} %collective-permute-done.3.refs_4_), channel_id=1, source_target_pairs={{0,1},{1,0},{2,3},{3,2},{4,5},{5,4},{6,7},{7,6},{8,9},{9,8},{10,11... | collective-permute-start | bytes 208904 | tf_op jit(solution)/shard_map/ppermute | solution.py:253
  18.4 1.6 %collective-permute-start.9 = (bf16[64,1024]{1,0:T(8,128)(2,1)S(1)}, bf16[64,1024]{1,0:T(8,128)(2,1)S(1)}, u32[]{:S(2)}, u32[]{:S(2)}) collective-permute-start(bf16[64,1024]{1,0:T(8,128)(2,1)S(1)} %get-tuple-element.18), channel_id=1, source_target_pairs={{0,1},{1,0},{2,3},{3,2},{4,5},{5,4},{6,7},{7,6},{8,9},{9,8},{10,11... | collective-permute-start | bytes 393224 | tf_op jit(solution)/shard_map/ppermute | solution.py:253
  18.6 6.5 %collective-permute-start.10 = (bf16[256,256]{1,0:T(8,128)(2,1)S(1)}, bf16[256,256]{1,0:T(8,128)(2,1)S(1)}, u32[]{:S(2)}, u32[]{:S(2)}) collective-permute-start(bf16[256,256]{1,0:T(8,128)(2,1)S(1)} %get-tuple-element.21), channel_id=1, source_target_pairs={{0,16},{16,0},{1,17},{17,1},{2,18},{18,2},{3,19},{19,3},{4,20},{20... | collective-permute-start | bytes 393224 | tf_op jit(solution)/shard_map/ppermute | solution.py:274
  19.1 7.5 %collective-permute-start.14 = (bf16[256,256]{1,0:T(8,128)(2,1)S(1)}, bf16[256,256]{1,0:T(8,128)(2,1)S(1)}, u32[]{:S(2)}, u32[]{:S(2)}) collective-permute-start(bf16[256,256]{1,0:T(8,128)(2,1)S(1)} %get-tuple-element.24), channel_id=1, source_target_pairs={{0,2},{1,3},{2,0},{3,1},{4,6},{5,7},{6,4},{7,5},{8,10},{9,11},{10,... | collective-permute-start | bytes 393224 | tf_op jit(solution)/shard_map/ppermute | solution.py:253
  20.1 6.6 %collective-permute-start.13 = (bf16[16,1024]{1,0:T(8,128)(2,1)S(1)}, bf16[16,1024]{1,0:T(8,128)(2,1)S(1)}, u32[]{:S(2)}, u32[]{:S(2)}) collective-permute-start(bf16[16,1024]{1,0:T(8,128)(2,1)S(1)} %get-tuple-element.27), channel_id=1, source_target_pairs={{0,12},{1,13},{2,14},{3,15},{4,8},{5,9},{6,10},{7,11},{8,4},{9,5},... | collective-permute-start | bytes 98312 | tf_op jit(solution)/shard_map/ppermute | solution.py:253
  23.2 5.2 %collective-permute-start.12 = (bf16[16,1024]{1,0:T(8,128)(2,1)S(1)}, bf16[16,1024]{1,0:T(8,128)(2,1)S(1)}, u32[]{:S(2)}, u32[]{:S(2)}) collective-permute-start(bf16[16,1024]{1,0:T(8,128)(2,1)S(1)} %get-tuple-element.28), channel_id=1, source_target_pairs={{0,8},{1,5},{2,10},{3,7},{4,12},{5,1},{6,14},{7,3},{8,0},{9,13},{1... | collective-permute-start | bytes 98312 | tf_op jit(solution)/shard_map/ppermute | solution.py:253
  23.2 5.9 %collective-permute-start.15 = (bf16[256,256]{1,0:T(8,128)(2,1)S(1)}, bf16[256,256]{1,0:T(8,128)(2,1)S(1)}, u32[]{:S(2)}, u32[]{:S(2)}) collective-permute-start(bf16[256,256]{1,0:T(8,128)(2,1)S(1)} %get-tuple-element.26), channel_id=1, source_target_pairs={{0,18},{1,19},{2,16},{3,17},{4,22},{5,23},{6,20},{7,21},{8,26},{9,... | collective-permute-start | bytes 393224 | tf_op jit(solution)/shard_map/ppermute | solution.py:282
  25.1 3.9 %collective-permute-start.11 = (bf16[16,1024]{1,0:T(8,128)(2,1)S(1)}, bf16[16,1024]{1,0:T(8,128)(2,1)S(1)}, u32[]{:S(2)}, u32[]{:S(2)}) collective-permute-start(bf16[16,1024]{1,0:T(8,128)(2,1)S(1)} %get-tuple-element.22), channel_id=1, source_target_pairs={{0,4},{1,9},{2,6},{3,11},{4,0},{5,13},{6,2},{7,15},{8,12},{9,1},{1... | collective-permute-start | bytes 98312 | tf_op jit(solution)/shard_map/ppermute | solution.py:253
